TPU v7x, 1024 devices: a whole 4x8x16 slice. The times are simulated.
1024 devices in a mesh: owner: 16 (over y, core), split: 16 (over z), rep: 4 (over x).
Axes of the slice: x: 4, y: 8, z: 16, core: 2. Of those that a mesh axis runs over, the one named last changes fastest.
Arguments:
- embeddings: bfloat16 [196608, 1024], P(('rep', 'owner', 'split')), parts along dimension 0, may hold values from -20 to 20
- cluster: int32 [196608], P(('rep', 'owner', 'split')), parts along dimension 0, may hold values from 0 to 15, as said below
- rank: int32 [196608], P(('rep', 'owner', 'split')), parts along dimension 0, may hold values from 0 to 49151, each once
Outputs:
- best: float32 [196608], P(('rep', 'owner', 'split')), parts along dimension 0
There are 4 independent parts, one for each index of `rep`. A program takes and returns all parts, laid end to end along the dimension named above; each array names one. Nothing has to cross between parts.
Inputs may be any that keep to these rules, and one draw needn't show every extreme that they name: `cluster`: cluster c belongs to owner index c mod 16. Among the 192 rows of one device at most 18 belong to clusters of one owner index, and exactly 18 for some owner index on every device.
All inputs are finite; a program needn't handle non-finite values.
Results may differ from a plain program's by a relative error of at most 0.00048.
Values may be sent and summed in bfloat16 or wider, within the bound.
No kernel may reach another device: no remote copies, remote signals or barrier semaphores. Data moves between devices by JAX's collectives and lax.ppermute only.
A program may use at most 32 MiB of HBM per device.

v0:
```python
import functools

import jax
import jax.numpy as jnp
from jax import lax
from jax.experimental import pallas as pl
from jax.experimental.pallas import tpu as pltpu
from jax.sharding import PartitionSpec as P

MAIN = 16
REM = 2
RANK_TILE = 8
LANES = 128
ABSENT = 256.0

NT = (((1,), (1,)), ((), ()))
NN = (((1,), (0,)), ((), ()))


def dot(left, right, dims):
    return lax.dot_general(left, right, dims, preferred_element_type=jnp.float32)


def iota(shape, dim):
    return lax.broadcasted_iota(jnp.int32, shape, dim)


def to_column(row):
    parts = []
    for at in range(0, row.shape[1], LANES):
        part = row[:, at : at + LANES]
        n = part.shape[1]
        same = iota((n, n), 0) == iota((n, n), 1)
        parts.append(jnp.sum(jnp.where(same, part, 0.0), axis=1, keepdims=True))
    return jnp.concatenate(parts, axis=0)


def to_row(column):
    parts = []
    for at in range(0, column.shape[0], LANES):
        part = column[at : at + LANES]
        n = part.shape[0]
        same = iota((n, n), 0) == iota((n, n), 1)
        parts.append(jnp.sum(jnp.where(same, part, 0.0), axis=0, keepdims=True))
    return jnp.concatenate(parts, axis=1)


def pack_kernel(groups, home_ref, emb_ref, cluster_ref, rank_ref, out_ref, place_ref):
    rows, width = emb_ref.shape
    pieces = width // LANES
    home = home_ref[0]
    wide = emb_ref[...].astype(jnp.float32)
    norm = jnp.sqrt(jnp.sum(wide * wide, axis=1, keepdims=True) + 1e-06)
    unit = (wide / norm).astype(jnp.bfloat16)

    target = lax.rem(cluster_ref[...], groups)
    target_column = to_column(target.astype(jnp.float32)).astype(jnp.int32)
    earlier = (target_column == target) & (iota((rows, rows), 0) < iota((rows, rows), 1))
    position = jnp.sum(earlier.astype(jnp.float32), axis=0, keepdims=True).astype(jnp.int32)
    is_main = position < MAIN
    place_ref[...] = jnp.where(
        is_main, home * MAIN + position, groups * MAIN + home * REM + position - MAIN
    )

    slot = jnp.where(is_main, target * MAIN + position, -1)
    placing = (iota((groups * MAIN, rows), 0) == slot).astype(jnp.bfloat16)
    main = dot(placing, unit, NN).astype(jnp.bfloat16)
    for k in range(pieces):
        piece = main[:, k * LANES : (k + 1) * LANES]
        out_ref[:, k * MAIN : (k + 1) * MAIN, :] = piece.reshape(groups, MAIN, LANES)

    spread = pieces * REM
    rest = jnp.zeros((groups * spread, LANES), jnp.float32)
    for k in range(pieces):
        slot = jnp.where(is_main, -1, target * spread + k * REM + position - MAIN)
        placing = (iota((groups * spread, rows), 0) == slot).astype(jnp.bfloat16)
        rest += dot(placing, unit[:, k * LANES : (k + 1) * LANES], NN)

    rank = rank_ref[...]
    high = (rank >> 8).astype(jnp.float32) - ABSENT
    low = (rank & 255).astype(jnp.float32)
    line = iota((groups * RANK_TILE, rows), 0)
    mine = line // RANK_TILE == target
    line = line % RANK_TILE
    band = home * MAIN // LANES
    lane = iota((LANES, rows), 0)
    at_main = (lane == jnp.where(is_main, lax.rem(home * MAIN, LANES) + position, -1)).astype(
        jnp.bfloat16
    )
    at_rest = (lane == jnp.where(is_main, -1, home * REM + position - MAIN)).astype(jnp.bfloat16)

    def values(first):
        value = jnp.where(line == first, high, jnp.where(line == first + 1, low, 0.0))
        return jnp.where(mine, value, 0.0).astype(jnp.bfloat16)

    tile = dot(values(2 * band), at_main, NT) + dot(values(4), at_rest, NT)
    shape = (groups * RANK_TILE, LANES)
    line, lane = iota(shape, 0) % RANK_TILE, iota(shape, 1)
    from_main = (line == 2 * band) & (lane // MAIN == lax.rem(home, LANES // MAIN))
    from_rest = (line == 4) & (lane // REM == home)
    tile += jnp.where(from_main | from_rest, ABSENT, 0.0)
    tail = jnp.concatenate(
        [rest.reshape(groups, spread, LANES), tile.reshape(groups, RANK_TILE, LANES)], axis=1
    )
    out_ref[:, pieces * MAIN :, :] = tail.astype(jnp.bfloat16)


def unpack(parts, scratch, slot):
    main_ref, rest_ref, main_rank_ref, rest_rank_ref = scratch
    width = main_ref.shape[2]
    pieces = width // LANES
    mains, rests, spread = main_ref.shape[1], rest_ref.shape[1], pieces * REM
    row, rest, tile = 0, [], 0.0
    for part in parts:
        senders = part.shape[0]
        for k in range(pieces):
            piece = part[:, k * MAIN : (k + 1) * MAIN, :].reshape(senders * MAIN, LANES)
            main_ref[slot, row : row + senders * MAIN, k * LANES : (k + 1) * LANES] = piece
        row += senders * MAIN
        tail = part[:, pieces * MAIN :, :].astype(jnp.float32)
        rest.append(tail[:, :spread, :].reshape(senders * spread, LANES).astype(jnp.bfloat16))
        tile = tile + jnp.sum(tail[:, spread:, :], axis=0)
    rest = jnp.concatenate(rest, axis=0) if len(rest) > 1 else rest[0]
    line, column = iota((pieces * rests, rest.shape[0]), 0), iota((pieces * rests, rest.shape[0]), 1)
    k, line = line // rests, line % rests
    pick = (column == line // REM * spread + k * REM + line % REM).astype(jnp.bfloat16)
    rest = dot(pick, rest, NN).astype(jnp.bfloat16)
    for k in range(pieces):
        rest_ref[slot, :, k * LANES : (k + 1) * LANES] = rest[k * rests : (k + 1) * rests]
    for g in range(mains // LANES):
        high, low = tile[2 * g : 2 * g + 1], tile[2 * g + 1 : 2 * g + 2]
        main_rank_ref[slot, :, g * LANES : (g + 1) * LANES] = high * 256.0 + low
    rest_rank_ref[slot] = (tile[4:5] * 256.0 + tile[5:6])[:, :rests]


def score(query, key, query_rank, key_rank):
    scores = dot(query, key, NT)
    lower = key_rank < query_rank
    return (
        jnp.max(jnp.where(lower, scores, -1.0), axis=1, keepdims=True),
        jnp.max(jnp.where(key_rank > query_rank, scores, -1.0), axis=0, keepdims=True),
    )


def meet(scratch, slots):
    main_ref, rest_ref, main_rank_ref, rest_rank_ref = scratch
    mains, rests, width = main_ref.shape[1], rest_ref.shape[1], main_ref.shape[2]
    others = slots - 1
    other = main_ref[1:slots].reshape(others * mains, width)
    other_rank = jnp.concatenate([to_column(main_rank_ref[i]) for i in range(1, slots)], axis=0)
    rest = rest_ref[0:slots].reshape(slots * rests, width)
    rest_row = jnp.concatenate([rest_rank_ref[i] for i in range(slots)], axis=1)
    rest_rank = to_column(rest_row)
    pivot, pivot_rank = main_ref[0], main_rank_ref[0]
    best_other, best_pivot = score(other, pivot, other_rank, pivot_rank)
    best_rest, found = score(rest, pivot, rest_rank, pivot_rank)
    best_pivot = jnp.maximum(best_pivot, found)
    found, back = score(other, rest_ref[0], other_rank, rest_row[:, :rests])
    best_other = jnp.maximum(best_other, found)
    best_rest = jnp.maximum(best_rest, score(rest, rest, rest_rank, rest_row)[0])
    best_rest = to_row(best_rest)
    results = [(best_pivot, jnp.maximum(best_rest[:, :rests], back))]
    for i in range(others):
        main = to_row(best_other[i * mains : (i + 1) * mains])
        results.append((main, best_rest[:, (i + 1) * rests : (i + 2) * rests]))
    return results


def keep(out_ref, results):
    for i, (main, rest) in enumerate(results):
        n = main.shape[1] + rest.shape[1]
        out_ref[i : i + 1, :n] = jnp.concatenate([main, rest], axis=1)


def near_kernel(own_ref, other_ref, ahead0_ref, ahead1_ref, out_ref, *scratch):
    main_ref, rest_ref, main_rank_ref, rest_rank_ref = scratch
    unpack([ahead0_ref, ahead1_ref], scratch, 0)
    unpack([own_ref], scratch, 1)
    unpack([other_ref], scratch, 2)
    results = meet(scratch, 3)
    rests, width = rest_ref.shape[1], main_ref.shape[2]
    own, own_rank = main_ref[1], to_column(main_rank_ref[1])
    (main_own, rest_own), (main_other, rest_other) = results[1:]
    own_best, _ = score(own, own, own_rank, main_rank_ref[1])
    found, _ = score(own, main_ref[2], own_rank, main_rank_ref[2])
    own_best = to_row(jnp.maximum(own_best, found))
    rest = rest_ref[1:3].reshape(2 * rests, width)
    rest_rank = to_column(jnp.concatenate([rest_rank_ref[1], rest_rank_ref[2]], axis=1))
    found, back = score(rest, own, rest_rank, main_rank_ref[1])
    found = to_row(found)
    main_own = jnp.maximum(jnp.maximum(main_own, own_best), back)
    rest_own = jnp.maximum(rest_own, found[:, :rests])
    found, back = score(rest_ref[1], main_ref[2], rest_rank[:rests], main_rank_ref[2])
    rest_own = jnp.maximum(rest_own, to_row(found))
    keep(out_ref, [results[0], (main_own, rest_own), (main_other, rest_other)])


def mid_kernel(own_ref, other_ref, ahead0_ref, ahead1_ref, back0_ref, back1_ref, out_ref, *scratch):
    unpack([back0_ref, back1_ref], scratch, 0)
    unpack([own_ref], scratch, 1)
    unpack([other_ref], scratch, 2)
    unpack([ahead0_ref, ahead1_ref], scratch, 3)
    keep(out_ref, meet(scratch, 4))


def late_kernel(
    place_ref, near_ref, mid_ref, back0_ref, back1_ref, far_back0_ref, far_back1_ref, far_ahead0_ref, far_ahead1_ref,
    out_ref, *scratch,
):
    unpack([back0_ref, back1_ref], scratch, 1)
    unpack([far_back0_ref, far_back1_ref], scratch, 2)
    unpack([far_ahead0_ref, far_ahead1_ref], scratch, 0)
    results = meet(scratch, 3)
    mains = results[0][0].shape[1]
    n = mains + results[0][1].shape[1]
    out_ref[...] = jnp.full(out_ref.shape, -1.0, jnp.float32)

    def add(i, values, start, end):
        at = (place_ref[i], slice(None), slice(start, end))
        out_ref[at] = jnp.maximum(out_ref[at], values)

    for i in range(3):
        add(i, near_ref[i : i + 1, :n], 0, n)
    for i in range(4):
        add(3 + i, mid_ref[i : i + 1, :n], 0, n)
    for i, (main, rest) in enumerate(results):
        add(7 + i, main, 0, mains)
        add(7 + i, rest, mains, n)


def pick_kernel(groups, arrived_ref, cluster_ref, place_ref, out_ref):
    arrived = arrived_ref[...].reshape(groups, arrived_ref.shape[2])
    rows = place_ref.shape[1]
    place = (iota((arrived.shape[1], rows), 0) == place_ref[...]).astype(jnp.bfloat16)
    found = jnp.zeros((groups, rows), jnp.float32)
    left = arrived
    for _ in range(3):
        term = left.astype(jnp.bfloat16)
        found += dot(term, place, NN)
        left = left - term.astype(jnp.float32)
    target = lax.rem(cluster_ref[...], groups)
    mine = iota((groups, rows), 0) == target
    out_ref[...] = jnp.sum(jnp.where(mine, found, 0.0), axis=0, keepdims=True)


def shards(embeddings, cluster, rank):
    rows, width = embeddings.shape
    owners, groups = lax.axis_size("owner"), lax.axis_size("split")
    pieces = width // LANES
    depth = pieces * (MAIN + REM) + RANK_TILE
    block_rows = groups * (MAIN + REM)
    padded = -(-block_rows // LANES) * LANES
    owner = lax.axis_index("owner").astype(jnp.int32)
    home = lax.axis_index("split").astype(jnp.int32)
    cluster, rank = cluster.reshape(1, rows), rank.reshape(1, rows)
    smem = pl.BlockSpec(memory_space=pltpu.SMEM)
    vmem = pl.BlockSpec(memory_space=pltpu.VMEM)
    params = pltpu.CompilerParams(vmem_limit_bytes=40 * 1024 * 1024)

    packed, slots = pl.pallas_call(
        functools.partial(pack_kernel, groups),
        out_shape=(
            jax.ShapeDtypeStruct((groups, depth, LANES), jnp.bfloat16),
            jax.ShapeDtypeStruct((1, rows), jnp.int32),
        ),
        in_specs=[smem, vmem, vmem, vmem],
        out_specs=(vmem, vmem),
        compiler_params=params,
        name="pack",
    )(home.reshape(1), embeddings, cluster, rank)

    block = lax.all_to_all(packed, "split", split_axis=0, concat_axis=0, tiled=True)

    chips = owners // 2

    def cross_ahead(chip):
        return (chip // (chips // 2)) & (chip % 2)

    def cross_back(chip):
        return 1 - cross_ahead((chip + chips - 1) % chips)

    def hop(value, step, cross):
        pairs = []
        for o in range(owners):
            to = (o // 2 + step) % chips
            pairs.append((o, to * 2 + (o % 2 ^ cross(to))))
        return lax.ppermute(value, "owner", pairs)

    def straight(chip):
        return 0

    def cut(large):
        return block[:large], block[large:]

    back = [hop(part, 1, straight) for part in cut(groups * 10 // 16)]
    ahead = [hop(part, -1, straight) for part in cut(groups * 9 // 16)]
    far_back = [hop(part, 1, cross_back) for part in back]
    far_ahead = [hop(part, -1, cross_ahead) for part in ahead]
    other = lax.ppermute(block, "owner", [(o, o ^ 1) for o in range(owners)])
    far_back[0], far_ahead[0] = lax.optimization_barrier((far_back[0], far_ahead[0]))

    chip, core = owner // 2, owner % 2

    def at(d, c):
        return lax.rem(chip + chips + d, chips) * 2 + c

    at_back, at_ahead = at(-1, core), at(1, core)
    at_far_back, at_far_ahead = at(-2, core ^ cross_back(chip)), at(2, core ^ cross_ahead(chip))
    place = jnp.stack(
        [at_ahead, owner, owner ^ 1]
        + [at_far_back, owner, owner ^ 1, at_ahead]
        + [at_far_ahead, at_back, at_far_back]
    )

    def call(kernel, out, slots, scalars, operands, name):
        return pl.pallas_call(
            kernel,
            out_shape=jax.ShapeDtypeStruct(out, jnp.float32),
            scratch_shapes=[
                pltpu.VMEM((slots, groups * MAIN, width), jnp.bfloat16),
                pltpu.VMEM((slots, groups * REM, width), jnp.bfloat16),
                pltpu.VMEM((slots, 1, groups * MAIN), jnp.float32),
                pltpu.VMEM((slots, 1, groups * REM), jnp.float32),
            ],
            in_specs=[smem] * scalars + [vmem] * operands,
            out_specs=vmem,
            compiler_params=params,
            cost_estimate=pl.CostEstimate(flops=1, bytes_accessed=1, transcendentals=0),
            name=name,
        )

    near = call(near_kernel, (8, padded), 3, 0, 4, "near")(block, other, *ahead)
    mid = call(mid_kernel, (8, padded), 4, 0, 6, "mid")(block, other, *ahead, *far_back)
    best = call(late_kernel, (owners, 1, padded), 3, 1, 8, "late")(
        place, near, mid, *back, *far_back, *far_ahead
    )

    best = lax.all_to_all(best, "owner", split_axis=0, concat_axis=0, tiled=True)
    best = jnp.broadcast_to(jnp.max(best, axis=0, keepdims=True), (groups, 1, padded))
    arrived = lax.all_to_all(best, "split", split_axis=0, concat_axis=0, tiled=True)

    result = pl.pallas_call(
        functools.partial(pick_kernel, groups),
        out_shape=jax.ShapeDtypeStruct((1, rows), jnp.float32),
        in_specs=[vmem, vmem, vmem],
        out_specs=vmem,
        compiler_params=params,
        name="pick",
    )(arrived, cluster, slots)
    return result.reshape(rows)


def solution(mesh):
    return jax.shard_map(
        shards,
        mesh=mesh,
        in_specs=(
            P(("rep", "owner", "split"), None),
            P(("rep", "owner", "split")),
            P(("rep", "owner", "split")),
        ),
        out_specs=P(("rep", "owner", "split")),
        check_vma=False,
    )
```

profile of v0, /device:TPU:6, one launch (start us, length us, event | category | flops | bytes accessed | tf_op | source)
XLA Modules:
  0.0 128.1 jit_solution(16547454990016818738)
XLA Ops:
  0.0 0.0 copy-start.2
  0.0 0.0 copy-start.1
  0.0 0.7 copy-done.2
  0.7 0.0 copy-done.1
  0.7 0.0 copy-start
  0.7 1.0 copy-done
  1.7 0.9 pack.1
  2.6 54.1 %all_to_all.15.own_ref = bf16[16,152,128]{2,1,0:T(8,128)(2,1)S(1)} all-to-all(bf16[16,152,128]{2,1,0:T(8,128)(2,1)S(1)} %get-tuple-element.9), channel_id=1, replica_groups=mesh['owner'=16,'split'=16,'rep'=4] {'split'}, dimensions={0} | all-to-all | bytes 1245184 | tf_op jit(solution)/shard_map/all_to_all | solution.py:272
  56.7 3.5 %collective-permute-start.3 = (bf16[10,152,128]{2,1,0:T(8,128)(2,1)S(1)}, bf16[10,152,128]{2,1,0:T(8,128)(2,1)S(1)}, u32[]{:S(2)}, u32[]{:S(2)}) collective-permute-start(bf16[10,152,128]{2,1,0:T(8,128)(2,1)S(1)} %slice.18), channel_id=1, source_target_pairs={{0,128},{64,192},{128,256},{192,320},{256,384},{320,448},{384,512}... | collective-permute-start | bytes 1167368 | tf_op jit(solution)/shard_map/ppermute | solution.py:287
  60.2 3.8 %collective-permute-start.1 = (bf16[9,152,128]{2,1,0:T(8,128)(2,1)S(1)}, bf16[9,152,128]{2,1,0:T(8,128)(2,1)S(1)}, u32[]{:S(2)}, u32[]{:S(2)}) collective-permute-start(bf16[9,152,128]{2,1,0:T(8,128)(2,1)S(1)} %slice.16), channel_id=1, source_target_pairs={{0,896},{64,960},{128,0},{192,64},{256,128},{320,192},{384,256},{4... | collective-permute-start | bytes 1050632 | tf_op jit(solution)/shard_map/ppermute | solution.py:287
  64.1 1.9 %collective-permute-start = (bf16[16,152,128]{2,1,0:T(8,128)(2,1)S(1)}, bf16[16,152,128]{2,1,0:T(8,128)(2,1)S(1)}, u32[]{:S(2)}, u32[]{:S(2)}) collective-permute-start(bf16[16,152,128]{2,1,0:T(8,128)(2,1)S(1)} %all_to_all.15.own_ref), channel_id=1, source_target_pairs={{0,64},{64,0},{128,192},{192,128},{256,320},{320,256},{384,448},{4... | collective-permute-start | bytes 1867784 | tf_op jit(solution)/shard_map/ppermute | solution.py:299
  66.0 3.9 %collective-permute-start.2 = (bf16[7,152,128]{2,1,0:T(8,128)(2,1)S(1)}, bf16[7,152,128]{2,1,0:T(8,128)(2,1)S(1)}, u32[]{:S(2)}, u32[]{:S(2)}) collective-permute-start(bf16[7,152,128]{2,1,0:T(8,128)(2,1)S(1)} %slice.17), channel_id=1, source_target_pairs={{0,896},{64,960},{128,0},{192,64},{256,128},{320,192},{384,256},{4... | collective-permute-start | bytes 817160 | tf_op jit(solution)/shard_map/ppermute | solution.py:287
  70.0 1.9 %collective-permute-start.6 = (bf16[6,152,128]{2,1,0:T(8,128)(2,1)S(1)}, bf16[6,152,128]{2,1,0:T(8,128)(2,1)}, u32[]{:S(2)}, u32[]{:S(2)}) collective-permute-start(bf16[6,152,128]{2,1,0:T(8,128)(2,1)S(1)} %slice.19), channel_id=1, source_target_pairs={{0,128},{64,192},{128,256},{192,320},{256,384},{320,448},{384,512}... | collective-permute-start | bytes 700424 | tf_op jit(solution)/shard_map/ppermute | solution.py:287
  71.9 0.0 collective-permute-done.3.back0_ref
  71.9 1.9 %collective-permute-start.4 = (bf16[10,152,128]{2,1,0:T(8,128)(2,1)S(1)}, bf16[10,152,128]{2,1,0:T(8,128)(2,1)S(1)}, u32[]{:S(2)}, u32[]{:S(2)}) collective-permute-start(bf16[10,152,128]{2,1,0:T(8,128)(2,1)S(1)} %collective-permute-done.3.back0_ref), channel_id=1, source_target_pairs={{0,192},{64,128},{128,320},{192,256},{256,448},{320,384},{384,576}... | collective-permute-start | bytes 1167368 | tf_op jit(solution)/shard_map/ppermute | solution.py:287
  73.8 0.0 collective-permute-done.1.ahead0_ref
  73.9 4.7 %collective-permute-start.5 = (bf16[9,152,128]{2,1,0:T(8,128)(2,1)S(1)}, bf16[9,152,128]{2,1,0:T(8,128)(2,1)S(1)}, u32[]{:S(2)}, u32[]{:S(2)}) collective-permute-start(bf16[9,152,128]{2,1,0:T(8,128)(2,1)S(1)} %collective-permute-done.1.ahead0_ref), channel_id=1, source_target_pairs={{0,960},{64,896},{128,0},{192,64},{256,128},{320,192},{384,256},{4... | collective-permute-start | bytes 1050632 | tf_op jit(solution)/shard_map/ppermute | solution.py:287
  78.5 0.0 collective-permute-done.2.ahead1_ref
  78.5 3.8 %collective-permute-start.8 = (bf16[7,152,128]{2,1,0:T(8,128)(2,1)S(1)}, bf16[7,152,128]{2,1,0:T(8,128)(2,1)S(1)}, u32[]{:S(2)}, u32[]{:S(2)}) collective-permute-start(bf16[7,152,128]{2,1,0:T(8,128)(2,1)S(1)} %collective-permute-done.2.ahead1_ref), channel_id=1, source_target_pairs={{0,960},{64,896},{128,0},{192,64},{256,128},{320,192},{384,256},{4... | collective-permute-start | bytes 817160 | tf_op jit(solution)/shard_map/ppermute | solution.py:287
  82.4 0.0 collective-permute-done.6.back1_ref
  82.4 1.9 %collective-permute-start.7 = (bf16[6,152,128]{2,1,0:T(8,128)(2,1)}, bf16[6,152,128]{2,1,0:T(8,128)(2,1)S(1)}, u32[]{:S(2)}, u32[]{:S(2)}) collective-permute-start(bf16[6,152,128]{2,1,0:T(8,128)(2,1)} %collective-permute-done.6.back1_ref), channel_id=1, source_target_pairs={{0,192},{64,128},{128,320},{192,256},{256,448},{320,384},{384,576}... | collective-permute-start | bytes 700424 | tf_op jit(solution)/shard_map/ppermute | solution.py:287
  84.4 0.1 stack.31.place_ref
  84.5 0.0 collective-permute-done.other_ref
  84.5 1.8 %near.1.near_ref = f32[8,384]{1,0:T(8,128)S(1)} custom-call(bf16[16,152,128]{2,1,0:T(8,128)(2,1)S(1)} %all_to_all.15.own_ref, bf16[16,152,128]{2,1,0:T(8,128)(2,1)S(1)} %collective-permute-done.other_ref, bf16[9,152,128]{2,1,0:T(8,128)(2,1)S(1)} %collective-permute-done.1.ahead0_ref, bf16[7,152,128]{2,1,0:T(8,128)(2,1)S(1)} %collective-permute-done.2.ahead1_ref), custom_call_target="tpu_custom_call" | custom-call | flops 1 | bytes 1 | tf_op jit(solution)/shard_map/near/pallas_call | solution.py:332
  86.4 0.7 collective-permute-done.5.far_ahead0_ref
  87.1 2.8 %collective-permute-done.4.back0_ref.far_back0_ref = bf16[10,152,128]{2,1,0:T(8,128)(2,1)S(1)} collective-permute-done((bf16[10,152,128]{2,1,0:T(8,128)(2,1)S(1)}, bf16[10,152,128]{2,1,0:T(8,128)(2,1)S(1)}, u32[]{:S(2)}, u32[]{:S(2)}) %collective-permute-start.4) | collective-permute-done | bytes 389152 | tf_op jit(solution)/shard_map/ppermute | solution.py:287
  89.9 4.3 %collective-permute-done.7.back1_ref.far_back1_ref = bf16[6,152,128]{2,1,0:T(8,128)(2,1)S(1)} collective-permute-done((bf16[6,152,128]{2,1,0:T(8,128)(2,1)}, bf16[6,152,128]{2,1,0:T(8,128)(2,1)S(1)}, u32[]{:S(2)}, u32[]{:S(2)}) %collective-permute-start.7) | collective-permute-done | bytes 233504 | tf_op jit(solution)/shard_map/ppermute | solution.py:287
  94.2 1.6 %mid.1.mid_ref = f32[8,384]{1,0:T(8,128)S(1)} custom-call(bf16[16,152,128]{2,1,0:T(8,128)(2,1)S(1)} %all_to_all.15.own_ref, bf16[16,152,128]{2,1,0:T(8,128)(2,1)S(1)} %collective-permute-done.other_ref, bf16[9,152,128]{2,1,0:T(8,128)(2,1)S(1)} %collective-permute-done.1.ahead0_ref, bf16[7,152,128]{2,1,0:T(8,128)(2,1)S(1)} %collective-permute-done.2.ahead1_ref, ...), custom_call_target="tpu_custom_call" | custom-call | flops 1 | bytes 1 | tf_op jit(solution)/shard_map/mid/pallas_call | solution.py:333
  95.8 0.0 collective-permute-done.8.far_ahead1_ref
  95.8 2.2 %late.1 = f32[16,1,384]{2,1,0:T(1,128)S(1)} custom-call(s32[10]{0:T(128)S(1)} %stack.31.place_ref, f32[8,384]{1,0:T(8,128)S(1)} %near.1.near_ref, f32[8,384]{1,0:T(8,128)S(1)} %mid.1.mid_ref, bf16[10,152,128]{2,1,0:T(8,128)(2,1)S(1)} %collective-permute-done.3.back0_ref, bf16[6,152,128]{2,1,0:T(8,128)(2,1)} %collective-permute-done.6.back1_ref, ...), custom_call_target="tpu_custom_call" | custom-call | flops 1 | bytes 1 | tf_op jit(solution)/shard_map/late/pallas_call | solution.py:334
  98.0 12.3 %all_to_all.16 = f32[16,1,384]{2,1,0:T(1,128)S(1)} all-to-all(f32[16,1,384]{2,1,0:T(1,128)S(1)} %late.1), channel_id=1, replica_groups=mesh['owner'=16,'split'=16,'rep'=4] {'owner'}, dimensions={0} | all-to-all | bytes 49152 | tf_op jit(solution)/shard_map/all_to_all | solution.py:338
  110.3 16.9 %all_to_all.17.arrived_ref = f32[16,1,384]{2,1,0:T(1,128)S(1)} all-to-all(f32[16,1,384]{2,1,0:T(1,128)S(1)} %broadcast_in_dim.2), channel_id=1, replica_groups=mesh['owner'=16,'split'=16,'rep'=4] {'split'}, dimensions={0} | all-to-all | bytes 49152 | tf_op jit(solution)/shard_map/all_to_all | solution.py:340
  127.3 0.9 pick.1
  (6 shorter events, 0.1 us)
Async XLA Ops:
  0.0 0.7 copy-start.2
  0.0 0.7 copy-start.1
  0.7 1.0 copy-start
  56.7 15.2 %collective-permute-start.3 = (bf16[10,152,128]{2,1,0:T(8,128)(2,1)S(1)}, bf16[10,152,128]{2,1,0:T(8,128)(2,1)S(1)}, u32[]{:S(2)}, u32[]{:S(2)}) collective-permute-start(bf16[10,152,128]{2,1,0:T(8,128)(2,1)S(1)} %slice.18), channel_id=1, source_target_pairs={{0,128},{64,192},{128,256},{192,320},{256,384},{320,448},{384,512}... | collective-permute-start | bytes 1167368 | tf_op jit(solution)/shard_map/ppermute | solution.py:287
  60.2 13.6 %collective-permute-start.1 = (bf16[9,152,128]{2,1,0:T(8,128)(2,1)S(1)}, bf16[9,152,128]{2,1,0:T(8,128)(2,1)S(1)}, u32[]{:S(2)}, u32[]{:S(2)}) collective-permute-start(bf16[9,152,128]{2,1,0:T(8,128)(2,1)S(1)} %slice.16), channel_id=1, source_target_pairs={{0,896},{64,960},{128,0},{192,64},{256,128},{320,192},{384,256},{4... | collective-permute-start | bytes 1050632 | tf_op jit(solution)/shard_map/ppermute | solution.py:287
  64.1 20.5 %collective-permute-start = (bf16[16,152,128]{2,1,0:T(8,128)(2,1)S(1)}, bf16[16,152,128]{2,1,0:T(8,128)(2,1)S(1)}, u32[]{:S(2)}, u32[]{:S(2)}) collective-permute-start(bf16[16,152,128]{2,1,0:T(8,128)(2,1)S(1)} %all_to_all.15.own_ref), channel_id=1, source_target_pairs={{0,64},{64,0},{128,192},{192,128},{256,320},{320,256},{384,448},{4... | collective-permute-start | bytes 1867784 | tf_op jit(solution)/shard_map/ppermute | solution.py:299
  66.0 12.5 %collective-permute-start.2 = (bf16[7,152,128]{2,1,0:T(8,128)(2,1)S(1)}, bf16[7,152,128]{2,1,0:T(8,128)(2,1)S(1)}, u32[]{:S(2)}, u32[]{:S(2)}) collective-permute-start(bf16[7,152,128]{2,1,0:T(8,128)(2,1)S(1)} %slice.17), channel_id=1, source_target_pairs={{0,896},{64,960},{128,0},{192,64},{256,128},{320,192},{384,256},{4... | collective-permute-start | bytes 817160 | tf_op jit(solution)/shard_map/ppermute | solution.py:287
  70.0 12.4 %collective-permute-start.6 = (bf16[6,152,128]{2,1,0:T(8,128)(2,1)S(1)}, bf16[6,152,128]{2,1,0:T(8,128)(2,1)}, u32[]{:S(2)}, u32[]{:S(2)}) collective-permute-start(bf16[6,152,128]{2,1,0:T(8,128)(2,1)S(1)} %slice.19), channel_id=1, source_target_pairs={{0,128},{64,192},{128,256},{192,320},{256,384},{320,448},{384,512}... | collective-permute-start | bytes 700424 | tf_op jit(solution)/shard_map/ppermute | solution.py:287
  71.9 18.0 %collective-permute-start.4 = (bf16[10,152,128]{2,1,0:T(8,128)(2,1)S(1)}, bf16[10,152,128]{2,1,0:T(8,128)(2,1)S(1)}, u32[]{:S(2)}, u32[]{:S(2)}) collective-permute-start(bf16[10,152,128]{2,1,0:T(8,128)(2,1)S(1)} %collective-permute-done.3.back0_ref), channel_id=1, source_target_pairs={{0,192},{64,128},{128,320},{192,256},{256,448},{320,384},{384,576}... | collective-permute-start | bytes 1167368 | tf_op jit(solution)/shard_map/ppermute | solution.py:287
  73.9 13.2 %collective-permute-start.5 = (bf16[9,152,128]{2,1,0:T(8,128)(2,1)S(1)}, bf16[9,152,128]{2,1,0:T(8,128)(2,1)S(1)}, u32[]{:S(2)}, u32[]{:S(2)}) collective-permute-start(bf16[9,152,128]{2,1,0:T(8,128)(2,1)S(1)} %collective-permute-done.1.ahead0_ref), channel_id=1, source_target_pairs={{0,960},{64,896},{128,0},{192,64},{256,128},{320,192},{384,256},{4... | collective-permute-start | bytes 1050632 | tf_op jit(solution)/shard_map/ppermute | solution.py:287
  78.5 17.2 %collective-permute-start.8 = (bf16[7,152,128]{2,1,0:T(8,128)(2,1)S(1)}, bf16[7,152,128]{2,1,0:T(8,128)(2,1)S(1)}, u32[]{:S(2)}, u32[]{:S(2)}) collective-permute-start(bf16[7,152,128]{2,1,0:T(8,128)(2,1)S(1)} %collective-permute-done.2.ahead1_ref), channel_id=1, source_target_pairs={{0,960},{64,896},{128,0},{192,64},{256,128},{320,192},{384,256},{4... | collective-permute-start | bytes 817160 | tf_op jit(solution)/shard_map/ppermute | solution.py:287
  82.4 11.9 %collective-permute-start.7 = (bf16[6,152,128]{2,1,0:T(8,128)(2,1)}, bf16[6,152,128]{2,1,0:T(8,128)(2,1)S(1)}, u32[]{:S(2)}, u32[]{:S(2)}) collective-permute-start(bf16[6,152,128]{2,1,0:T(8,128)(2,1)} %collective-permute-done.6.back1_ref), channel_id=1, source_target_pairs={{0,192},{64,128},{128,320},{192,256},{256,448},{320,384},{384,576}... | collective-permute-start | bytes 700424 | tf_op jit(solution)/shard_map/ppermute | solution.py:287
where the time goes:
time: 129 us; the launch traced here: 128 us
  blocking collectives  83.3 us (65%)
  starting transfers between devices  27.4 us (21%)
  waiting for transfers between devices  7.89 us (6%)
  Pallas kernels  7.31 us (6%)
  local copies, waits for them, and re-layouts  1.89 us (1%)
    all_to_all x1, blocking collectives, shards(): lax.all_to_all(packed, 'split', split_axis=0, concat_axis=0, tiled=True)  54.1 us
    ppermute x8, starting transfers between devices, hop(): return lax.ppermute(value, 'owner', pairs)  25.5 us
    all_to_all x1, blocking collectives, shards(): lax.all_to_all(best, 'split', split_axis=0, concat_axis=0, tiled=True)  16.9 us
    all_to_all x1, blocking collectives, shards(): lax.all_to_all(best, 'owner', split_axis=0, concat_axis=0, tiled=True)  12.3 us
    ppermute x8, waiting for transfers between devices, hop(): return lax.ppermute(value, 'owner', pairs)  7.89 us
  transfers between devices with their start and end apart: 9, of which 3 were waited for; matrix products, arithmetic and copies ran while one was open for 0% of the time, Pallas kernels for 3%

commit v1 on v0

--- a/solution.py
+++ b/solution.py
@@ -138,7 +138,7 @@
     lower = key_rank < query_rank
     return (
         jnp.max(jnp.where(lower, scores, -1.0), axis=1, keepdims=True),
-        jnp.max(jnp.where(key_rank > query_rank, scores, -1.0), axis=0, keepdims=True),
+        jnp.max(jnp.where(lower, -1.0, scores), axis=0, keepdims=True),
     )
 
 
@@ -207,12 +207,12 @@
     place_ref, near_ref, mid_ref, back0_ref, back1_ref, far_back0_ref, far_back1_ref, far_ahead0_ref, far_ahead1_ref,
     out_ref, *scratch,
 ):
+    main_ref, rest_ref, _, _ = scratch
     unpack([back0_ref, back1_ref], scratch, 1)
     unpack([far_back0_ref, far_back1_ref], scratch, 2)
     unpack([far_ahead0_ref, far_ahead1_ref], scratch, 0)
-    results = meet(scratch, 3)
-    mains = results[0][0].shape[1]
-    n = mains + results[0][1].shape[1]
+    mains = main_ref.shape[1]
+    n = mains + rest_ref.shape[1]
     out_ref[...] = jnp.full(out_ref.shape, -1.0, jnp.float32)
 
     def add(i, values, start, end):
@@ -223,7 +223,7 @@
         add(i, near_ref[i : i + 1, :n], 0, n)
     for i in range(4):
         add(3 + i, mid_ref[i : i + 1, :n], 0, n)
-    for i, (main, rest) in enumerate(results):
+    for i, (main, rest) in enumerate(meet(scratch, 3)):
         add(7 + i, main, 0, mains)
         add(7 + i, rest, mains, n)
 

time: 129 us -> 129 us (level)
  no operation moved by 1% of the time
where the time goes in v1:
time: 129 us; the launch traced here: 128 us
  blocking collectives  83.3 us (65%)
  starting transfers between devices  27.4 us (21%)
  waiting for transfers between devices  7.89 us (6%)
  Pallas kernels  7.31 us (6%)
  local copies, waits for them, and re-layouts  1.89 us (1%)
    all_to_all x1, blocking collectives, shards(): lax.all_to_all(packed, 'split', split_axis=0, concat_axis=0, tiled=True)  54.1 us
    ppermute x8, starting transfers between devices, hop(): return lax.ppermute(value, 'owner', pairs)  25.5 us
    all_to_all x1, blocking collectives, shards(): lax.all_to_all(best, 'split', split_axis=0, concat_axis=0, tiled=True)  16.9 us
    all_to_all x1, blocking collectives, shards(): lax.all_to_all(best, 'owner', split_axis=0, concat_axis=0, tiled=True)  12.3 us
    ppermute x8, waiting for transfers between devices, hop(): return lax.ppermute(value, 'owner', pairs)  7.89 us
  transfers between devices with their start and end apart: 9, of which 3 were waited for; matrix products, arithmetic and copies ran while one was open for 0% of the time, Pallas kernels for 3%

profile of v1, /device:TPU:6, one launch (start us, length us, event | category | flops | bytes accessed | tf_op | source)
XLA Modules:
  0.0 128.1 jit_solution(10669571424976563669)
XLA Ops:
  0.0 0.0 copy-start.2
  0.0 0.0 copy-start.1
  0.0 0.7 copy-done.2
  0.7 0.0 copy-done.1
  0.7 0.0 copy-start
  0.7 1.0 copy-done
  1.7 0.9 pack.1
  2.6 54.1 %all_to_all.15.own_ref = bf16[16,152,128]{2,1,0:T(8,128)(2,1)S(1)} all-to-all(bf16[16,152,128]{2,1,0:T(8,128)(2,1)S(1)} %get-tuple-element.9), channel_id=1, replica_groups=mesh['owner'=16,'split'=16,'rep'=4] {'split'}, dimensions={0} | all-to-all | bytes 1245184 | tf_op jit(solution)/shard_map/all_to_all | solution.py:272
  56.7 3.5 %collective-permute-start.3 = (bf16[10,152,128]{2,1,0:T(8,128)(2,1)S(1)}, bf16[10,152,128]{2,1,0:T(8,128)(2,1)S(1)}, u32[]{:S(2)}, u32[]{:S(2)}) collective-permute-start(bf16[10,152,128]{2,1,0:T(8,128)(2,1)S(1)} %slice.18), channel_id=1, source_target_pairs={{0,128},{64,192},{128,256},{192,320},{256,384},{320,448},{384,512}... | collective-permute-start | bytes 1167368 | tf_op jit(solution)/shard_map/ppermute | solution.py:287
  60.2 3.8 %collective-permute-start.1 = (bf16[9,152,128]{2,1,0:T(8,128)(2,1)S(1)}, bf16[9,152,128]{2,1,0:T(8,128)(2,1)S(1)}, u32[]{:S(2)}, u32[]{:S(2)}) collective-permute-start(bf16[9,152,128]{2,1,0:T(8,128)(2,1)S(1)} %slice.16), channel_id=1, source_target_pairs={{0,896},{64,960},{128,0},{192,64},{256,128},{320,192},{384,256},{4... | collective-permute-start | bytes 1050632 | tf_op jit(solution)/shard_map/ppermute | solution.py:287
  64.1 1.9 %collective-permute-start = (bf16[16,152,128]{2,1,0:T(8,128)(2,1)S(1)}, bf16[16,152,128]{2,1,0:T(8,128)(2,1)S(1)}, u32[]{:S(2)}, u32[]{:S(2)}) collective-permute-start(bf16[16,152,128]{2,1,0:T(8,128)(2,1)S(1)} %all_to_all.15.own_ref), channel_id=1, source_target_pairs={{0,64},{64,0},{128,192},{192,128},{256,320},{320,256},{384,448},{4... | collective-permute-start | bytes 1867784 | tf_op jit(solution)/shard_map/ppermute | solution.py:299
  66.0 3.9 %collective-permute-start.2 = (bf16[7,152,128]{2,1,0:T(8,128)(2,1)S(1)}, bf16[7,152,128]{2,1,0:T(8,128)(2,1)S(1)}, u32[]{:S(2)}, u32[]{:S(2)}) collective-permute-start(bf16[7,152,128]{2,1,0:T(8,128)(2,1)S(1)} %slice.17), channel_id=1, source_target_pairs={{0,896},{64,960},{128,0},{192,64},{256,128},{320,192},{384,256},{4... | collective-permute-start | bytes 817160 | tf_op jit(solution)/shard_map/ppermute | solution.py:287
  70.0 1.9 %collective-permute-start.6 = (bf16[6,152,128]{2,1,0:T(8,128)(2,1)S(1)}, bf16[6,152,128]{2,1,0:T(8,128)(2,1)}, u32[]{:S(2)}, u32[]{:S(2)}) collective-permute-start(bf16[6,152,128]{2,1,0:T(8,128)(2,1)S(1)} %slice.19), channel_id=1, source_target_pairs={{0,128},{64,192},{128,256},{192,320},{256,384},{320,448},{384,512}... | collective-permute-start | bytes 700424 | tf_op jit(solution)/shard_map/ppermute | solution.py:287
  71.9 0.0 collective-permute-done.3.back0_ref
  71.9 1.9 %collective-permute-start.4 = (bf16[10,152,128]{2,1,0:T(8,128)(2,1)S(1)}, bf16[10,152,128]{2,1,0:T(8,128)(2,1)S(1)}, u32[]{:S(2)}, u32[]{:S(2)}) collective-permute-start(bf16[10,152,128]{2,1,0:T(8,128)(2,1)S(1)} %collective-permute-done.3.back0_ref), channel_id=1, source_target_pairs={{0,192},{64,128},{128,320},{192,256},{256,448},{320,384},{384,576}... | collective-permute-start | bytes 1167368 | tf_op jit(solution)/shard_map/ppermute | solution.py:287
  73.8 0.0 collective-permute-done.1.ahead0_ref
  73.9 4.7 %collective-permute-start.5 = (bf16[9,152,128]{2,1,0:T(8,128)(2,1)S(1)}, bf16[9,152,128]{2,1,0:T(8,128)(2,1)S(1)}, u32[]{:S(2)}, u32[]{:S(2)}) collective-permute-start(bf16[9,152,128]{2,1,0:T(8,128)(2,1)S(1)} %collective-permute-done.1.ahead0_ref), channel_id=1, source_target_pairs={{0,960},{64,896},{128,0},{192,64},{256,128},{320,192},{384,256},{4... | collective-permute-start | bytes 1050632 | tf_op jit(solution)/shard_map/ppermute | solution.py:287
  78.5 0.0 collective-permute-done.2.ahead1_ref
  78.5 3.8 %collective-permute-start.8 = (bf16[7,152,128]{2,1,0:T(8,128)(2,1)S(1)}, bf16[7,152,128]{2,1,0:T(8,128)(2,1)S(1)}, u32[]{:S(2)}, u32[]{:S(2)}) collective-permute-start(bf16[7,152,128]{2,1,0:T(8,128)(2,1)S(1)} %collective-permute-done.2.ahead1_ref), channel_id=1, source_target_pairs={{0,960},{64,896},{128,0},{192,64},{256,128},{320,192},{384,256},{4... | collective-permute-start | bytes 817160 | tf_op jit(solution)/shard_map/ppermute | solution.py:287
  82.4 0.0 collective-permute-done.6.back1_ref
  82.4 1.9 %collective-permute-start.7 = (bf16[6,152,128]{2,1,0:T(8,128)(2,1)}, bf16[6,152,128]{2,1,0:T(8,128)(2,1)S(1)}, u32[]{:S(2)}, u32[]{:S(2)}) collective-permute-start(bf16[6,152,128]{2,1,0:T(8,128)(2,1)} %collective-permute-done.6.back1_ref), channel_id=1, source_target_pairs={{0,192},{64,128},{128,320},{192,256},{256,448},{320,384},{384,576}... | collective-permute-start | bytes 700424 | tf_op jit(solution)/shard_map/ppermute | solution.py:287
  84.4 0.1 stack.31.place_ref
  84.5 0.0 collective-permute-done.other_ref
  84.5 1.8 %near.1.near_ref = f32[8,384]{1,0:T(8,128)S(1)} custom-call(bf16[16,152,128]{2,1,0:T(8,128)(2,1)S(1)} %all_to_all.15.own_ref, bf16[16,152,128]{2,1,0:T(8,128)(2,1)S(1)} %collective-permute-done.other_ref, bf16[9,152,128]{2,1,0:T(8,128)(2,1)S(1)} %collective-permute-done.1.ahead0_ref, bf16[7,152,128]{2,1,0:T(8,128)(2,1)S(1)} %collective-permute-done.2.ahead1_ref), custom_call_target="tpu_custom_call" | custom-call | flops 1 | bytes 1 | tf_op jit(solution)/shard_map/near/pallas_call | solution.py:332
  86.4 0.7 collective-permute-done.5.far_ahead0_ref
  87.1 2.8 %collective-permute-done.4.back0_ref.far_back0_ref = bf16[10,152,128]{2,1,0:T(8,128)(2,1)S(1)} collective-permute-done((bf16[10,152,128]{2,1,0:T(8,128)(2,1)S(1)}, bf16[10,152,128]{2,1,0:T(8,128)(2,1)S(1)}, u32[]{:S(2)}, u32[]{:S(2)}) %collective-permute-start.4) | collective-permute-done | bytes 389152 | tf_op jit(solution)/shard_map/ppermute | solution.py:287
  89.9 4.3 %collective-permute-done.7.back1_ref.far_back1_ref = bf16[6,152,128]{2,1,0:T(8,128)(2,1)S(1)} collective-permute-done((bf16[6,152,128]{2,1,0:T(8,128)(2,1)}, bf16[6,152,128]{2,1,0:T(8,128)(2,1)S(1)}, u32[]{:S(2)}, u32[]{:S(2)}) %collective-permute-start.7) | collective-permute-done | bytes 233504 | tf_op jit(solution)/shard_map/ppermute | solution.py:287
  94.2 1.5 %mid.1.mid_ref = f32[8,384]{1,0:T(8,128)S(1)} custom-call(bf16[16,152,128]{2,1,0:T(8,128)(2,1)S(1)} %all_to_all.15.own_ref, bf16[16,152,128]{2,1,0:T(8,128)(2,1)S(1)} %collective-permute-done.other_ref, bf16[9,152,128]{2,1,0:T(8,128)(2,1)S(1)} %collective-permute-done.1.ahead0_ref, bf16[7,152,128]{2,1,0:T(8,128)(2,1)S(1)} %collective-permute-done.2.ahead1_ref, ...), custom_call_target="tpu_custom_call" | custom-call | flops 1 | bytes 1 | tf_op jit(solution)/shard_map/mid/pallas_call | solution.py:333
  95.8 0.0 collective-permute-done.8.far_ahead1_ref
  95.8 2.2 %late.1 = f32[16,1,384]{2,1,0:T(1,128)S(1)} custom-call(s32[10]{0:T(128)S(1)} %stack.31.place_ref, f32[8,384]{1,0:T(8,128)S(1)} %near.1.near_ref, f32[8,384]{1,0:T(8,128)S(1)} %mid.1.mid_ref, bf16[10,152,128]{2,1,0:T(8,128)(2,1)S(1)} %collective-permute-done.3.back0_ref, bf16[6,152,128]{2,1,0:T(8,128)(2,1)} %collective-permute-done.6.back1_ref, ...), custom_call_target="tpu_custom_call" | custom-call | flops 1 | bytes 1 | tf_op jit(solution)/shard_map/late/pallas_call | solution.py:334
  98.0 12.3 %all_to_all.16 = f32[16,1,384]{2,1,0:T(1,128)S(1)} all-to-all(f32[16,1,384]{2,1,0:T(1,128)S(1)} %late.1), channel_id=1, replica_groups=mesh['owner'=16,'split'=16,'rep'=4] {'owner'}, dimensions={0} | all-to-all | bytes 49152 | tf_op jit(solution)/shard_map/all_to_all | solution.py:338
  110.3 16.9 %all_to_all.17.arrived_ref = f32[16,1,384]{2,1,0:T(1,128)S(1)} all-to-all(f32[16,1,384]{2,1,0:T(1,128)S(1)} %broadcast_in_dim.2), channel_id=1, replica_groups=mesh['owner'=16,'split'=16,'rep'=4] {'split'}, dimensions={0} | all-to-all | bytes 49152 | tf_op jit(solution)/shard_map/all_to_all | solution.py:340
  127.3 0.9 pick.1
  (6 shorter events, 0.1 us)
Async XLA Ops:
  0.0 0.7 copy-start.2
  0.0 0.7 copy-start.1
  0.7 1.0 copy-start
  56.7 15.2 %collective-permute-start.3 = (bf16[10,152,128]{2,1,0:T(8,128)(2,1)S(1)}, bf16[10,152,128]{2,1,0:T(8,128)(2,1)S(1)}, u32[]{:S(2)}, u32[]{:S(2)}) collective-permute-start(bf16[10,152,128]{2,1,0:T(8,128)(2,1)S(1)} %slice.18), channel_id=1, source_target_pairs={{0,128},{64,192},{128,256},{192,320},{256,384},{320,448},{384,512}... | collective-permute-start | bytes 1167368 | tf_op jit(solution)/shard_map/ppermute | solution.py:287
  60.2 13.6 %collective-permute-start.1 = (bf16[9,152,128]{2,1,0:T(8,128)(2,1)S(1)}, bf16[9,152,128]{2,1,0:T(8,128)(2,1)S(1)}, u32[]{:S(2)}, u32[]{:S(2)}) collective-permute-start(bf16[9,152,128]{2,1,0:T(8,128)(2,1)S(1)} %slice.16), channel_id=1, source_target_pairs={{0,896},{64,960},{128,0},{192,64},{256,128},{320,192},{384,256},{4... | collective-permute-start | bytes 1050632 | tf_op jit(solution)/shard_map/ppermute | solution.py:287
  64.1 20.5 %collective-permute-start = (bf16[16,152,128]{2,1,0:T(8,128)(2,1)S(1)}, bf16[16,152,128]{2,1,0:T(8,128)(2,1)S(1)}, u32[]{:S(2)}, u32[]{:S(2)}) collective-permute-start(bf16[16,152,128]{2,1,0:T(8,128)(2,1)S(1)} %all_to_all.15.own_ref), channel_id=1, source_target_pairs={{0,64},{64,0},{128,192},{192,128},{256,320},{320,256},{384,448},{4... | collective-permute-start | bytes 1867784 | tf_op jit(solution)/shard_map/ppermute | solution.py:299
  66.0 12.5 %collective-permute-start.2 = (bf16[7,152,128]{2,1,0:T(8,128)(2,1)S(1)}, bf16[7,152,128]{2,1,0:T(8,128)(2,1)S(1)}, u32[]{:S(2)}, u32[]{:S(2)}) collective-permute-start(bf16[7,152,128]{2,1,0:T(8,128)(2,1)S(1)} %slice.17), channel_id=1, source_target_pairs={{0,896},{64,960},{128,0},{192,64},{256,128},{320,192},{384,256},{4... | collective-permute-start | bytes 817160 | tf_op jit(solution)/shard_map/ppermute | solution.py:287
  70.0 12.4 %collective-permute-start.6 = (bf16[6,152,128]{2,1,0:T(8,128)(2,1)S(1)}, bf16[6,152,128]{2,1,0:T(8,128)(2,1)}, u32[]{:S(2)}, u32[]{:S(2)}) collective-permute-start(bf16[6,152,128]{2,1,0:T(8,128)(2,1)S(1)} %slice.19), channel_id=1, source_target_pairs={{0,128},{64,192},{128,256},{192,320},{256,384},{320,448},{384,512}... | collective-permute-start | bytes 700424 | tf_op jit(solution)/shard_map/ppermute | solution.py:287
  71.9 18.0 %collective-permute-start.4 = (bf16[10,152,128]{2,1,0:T(8,128)(2,1)S(1)}, bf16[10,152,128]{2,1,0:T(8,128)(2,1)S(1)}, u32[]{:S(2)}, u32[]{:S(2)}) collective-permute-start(bf16[10,152,128]{2,1,0:T(8,128)(2,1)S(1)} %collective-permute-done.3.back0_ref), channel_id=1, source_target_pairs={{0,192},{64,128},{128,320},{192,256},{256,448},{320,384},{384,576}... | collective-permute-start | bytes 1167368 | tf_op jit(solution)/shard_map/ppermute | solution.py:287
  73.9 13.2 %collective-permute-start.5 = (bf16[9,152,128]{2,1,0:T(8,128)(2,1)S(1)}, bf16[9,152,128]{2,1,0:T(8,128)(2,1)S(1)}, u32[]{:S(2)}, u32[]{:S(2)}) collective-permute-start(bf16[9,152,128]{2,1,0:T(8,128)(2,1)S(1)} %collective-permute-done.1.ahead0_ref), channel_id=1, source_target_pairs={{0,960},{64,896},{128,0},{192,64},{256,128},{320,192},{384,256},{4... | collective-permute-start | bytes 1050632 | tf_op jit(solution)/shard_map/ppermute | solution.py:287
  78.5 17.2 %collective-permute-start.8 = (bf16[7,152,128]{2,1,0:T(8,128)(2,1)S(1)}, bf16[7,152,128]{2,1,0:T(8,128)(2,1)S(1)}, u32[]{:S(2)}, u32[]{:S(2)}) collective-permute-start(bf16[7,152,128]{2,1,0:T(8,128)(2,1)S(1)} %collective-permute-done.2.ahead1_ref), channel_id=1, source_target_pairs={{0,960},{64,896},{128,0},{192,64},{256,128},{320,192},{384,256},{4... | collective-permute-start | bytes 817160 | tf_op jit(solution)/shard_map/ppermute | solution.py:287
  82.4 11.9 %collective-permute-start.7 = (bf16[6,152,128]{2,1,0:T(8,128)(2,1)}, bf16[6,152,128]{2,1,0:T(8,128)(2,1)S(1)}, u32[]{:S(2)}, u32[]{:S(2)}) collective-permute-start(bf16[6,152,128]{2,1,0:T(8,128)(2,1)} %collective-permute-done.6.back1_ref), channel_id=1, source_target_pairs={{0,192},{64,128},{128,320},{192,256},{256,448},{320,384},{384,576}... | collective-permute-start | bytes 700424 | tf_op jit(solution)/shard_map/ppermute | solution.py:287
